TPU v7x, 512 devices: a whole 4x4x16 slice. The times are simulated.
512 devices in a mesh: row: 32 (over z_hi, y, core), chan: 16 (over z_lo, x).
Axes of the slice: x: 4, y: 4, z: 16 (z_hi: 4, z_lo: 4; z = z_hi * 4 + z_lo), core: 2. Of those that a mesh axis runs over, the one named last changes fastest.
Arguments:
- features: bfloat16 [1, 256, 256, 256], P(None, 'chan', 'row'), may hold values from -6 to 6
- pre_act: bfloat16 [1, 512, 128, 128], P(None, 'chan', 'row'), may hold values from -6 to 6
- cotangent: bfloat16 [1, 512, 128, 128], P(None, 'chan', 'row'), may hold values from -6 to 6
- w_strided: bfloat16 [4, 4, 256, 512], P(None, None, 'chan'), may hold values from -0.09375 to 0.09375
- w_square: bfloat16 [3, 3, 512, 512], P(None, None, 'chan'), may hold values from -0.09375 to 0.09375
Outputs:
- grad_features: bfloat16 [1, 256, 256, 256], P(None, 'chan', 'row')
- grad_w_strided: float32 [4, 4, 256, 512], P(None, None, 'chan', 'row')
- grad_w_square: float32 [3, 3, 512, 512], P(None, None, 'chan', 'row')
All inputs are finite; a program needn't handle non-finite values.
Results may differ from a plain program's by a relative error of at most 0.0049.
Values may be sent and summed in bfloat16 or wider, within the bound.
A program may use at most 64 MiB of HBM per device.

v0:
```python
import math

import jax
import jax.numpy as jnp
from jax import lax
from jax.sharding import PartitionSpec as P


def padded_2(block, sides, width):
    for axis, dim in sides:
        count = lax.axis_size(axis)
        forward = [(i, i + 1) for i in range(count - 1)]
        backward = [(target, source) for source, target in forward]
        low = lax.ppermute(
            lax.slice_in_dim(block, block.shape[dim] - width, None, axis=dim), axis, forward
        )
        high = lax.ppermute(lax.slice_in_dim(block, 0, width, axis=dim), axis, backward)
        block = jnp.concatenate([low, block, high], axis=dim)
    return block


def body(features, pre_act, cotangent, w_strided, w_square):
    batch_size = features.shape[0]
    cin_local = features.shape[1]
    hid_local = pre_act.shape[1]
    out_rows = pre_act.shape[2]
    out_cols = pre_act.shape[3]
    channels = w_square.shape[3]
    grad_scale = 1.0 / math.sqrt(batch_size * out_rows * lax.axis_size("row") * out_cols)
    active = jnp.maximum(pre_act, 0)
    gathered = lax.all_gather(cotangent, "chan", axis=1, tiled=True)
    rimmed = padded_2(gathered, (("row", 2),), 1)
    grad_lower = jnp.zeros((batch_size, hid_local, out_rows, out_cols), jnp.float32)
    kernel_grad = jnp.zeros((3, 3, hid_local, channels), jnp.float32)
    padded = jnp.pad(rimmed, ((0, 0), (0, 0), (0, 0), (1, 1)))
    for tap_row in range(3):
        for tap_col in range(3):
            window = padded[
                :, :, 2 - tap_row : 2 - tap_row + out_rows, 2 - tap_col : 2 - tap_col + out_cols
            ]
            kernel = w_square[tap_row, tap_col]
            grad_lower = grad_lower + jnp.einsum(
                "bdhw,cd->bchw", window, kernel, preferred_element_type=jnp.float32
            )
            tap_sum = jnp.einsum(
                "bchw,bdhw->cd", active, window, preferred_element_type=jnp.float32
            )
            before_sum = kernel_grad[tap_row, tap_col]
            updated = before_sum + tap_sum
            kernel_grad = kernel_grad.at[tap_row, tap_col].set(updated)
    square_grad = kernel_grad
    grad_hidden = jnp.where(pre_act > 0, grad_lower, 0.0).astype(jnp.bfloat16)
    gathered_hidden = lax.all_gather(grad_hidden, "chan", axis=1, tiled=True)
    rimmed_hidden = padded_2(gathered_hidden, (("row", 2),), 1)
    phases = jnp.zeros((2, 2, batch_size, cin_local, out_rows, out_cols), jnp.float32)
    kernel_grad = jnp.zeros((4, 4, cin_local, channels), jnp.float32)
    padded = jnp.pad(rimmed_hidden, ((0, 0), (0, 0), (0, 0), (1, 1)))
    for row_phase in range(2):
        for col_phase in range(2):
            pixels = features[:, :, row_phase::2, col_phase::2]
            for tap_row in ((row_phase + 1) % 2, (row_phase + 1) % 2 + 2):
                row_first = (row_phase + 3 - tap_row) // 2
                for tap_col in ((col_phase + 1) % 2, (col_phase + 1) % 2 + 2):
                    col_first = (col_phase + 3 - tap_col) // 2
                    window = padded[
                        :, :, row_first : row_first + out_rows, col_first : col_first + out_cols
                    ]
                    kernel = w_strided[tap_row, tap_col]
                    phase_term = jnp.einsum(
                        "bdhw,cd->bchw", window, kernel, preferred_element_type=jnp.float32
                    )
                    phases = phases.at[row_phase, col_phase].add(phase_term)
                    tap_sum = jnp.einsum(
                        "bchw,bdhw->cd", pixels, window, preferred_element_type=jnp.float32
                    )
                    before_sum = kernel_grad[tap_row, tap_col]
                    updated = before_sum + tap_sum
                    kernel_grad = kernel_grad.at[tap_row, tap_col].set(updated)
    phases, strided_grad = (phases, kernel_grad)
    grad_features = (
        jnp.transpose(phases, (2, 3, 4, 0, 5, 1)).reshape(features.shape).astype(jnp.bfloat16)
    )
    strided_out, square_out = (
        lax.psum_scatter(strided_grad * grad_scale, "row", scatter_dimension=3, tiled=True),
        lax.psum_scatter(square_grad * grad_scale, "row", scatter_dimension=3, tiled=True),
    )
    return (grad_features, strided_out, square_out)


def solution(mesh):
    in_specs = (
        P(None, "chan", "row", None),
        P(None, "chan", "row", None),
        P(None, "chan", "row", None),
        P(None, None, "chan", None),
        P(None, None, "chan", None),
    )
    out_specs = (
        P(None, "chan", "row", None),
        P(None, None, "chan", "row"),
        P(None, None, "chan", "row"),
    )
    return jax.shard_map(body, mesh=mesh, in_specs=in_specs, out_specs=out_specs, check_vma=False)
```

profile of v0, /device:TPU:24, one launch (start us, length us, event | category | flops | bytes accessed | tf_op | source)
XLA Modules:
  0.0 632.2 jit_solution(15049788761735872323)
XLA Ops:
  8.0 46.5 %all_gather.6 = bf16[1,512,4,128]{3,1,2,0:T(8,128)(2,1)S(1)} all-gather(bf16[1,32,4,128]{3,1,2,0:T(8,128)(2,1)S(1)} %copy.27), channel_id=1, replica_groups=mesh['row'=32,'chan'=16] {'chan'}, dimensions={1}, use_global_device_ids=true | all-gather | bytes 557056 | tf_op jit(solution)/shard_map/all_gather | solution.py:31
  54.5 2.1 collective-permute-start
  56.5 3.6 collective-permute-start.1
  62.1 2.6 slice.1591
  64.7 2.6 slice.1586
  67.3 2.0 slice.1582
  69.3 2.0 slice.1598
  71.3 1.3 dynamic-slice.343
  73.2 1.5 and_reduce_fusion
  74.7 0.8 select_maximum_fusion.2
  78.1 39.9 %all_gather.7 = bf16[1,512,4,128]{3,1,2,0:T(8,128)(2,1)S(1)} all-gather(bf16[1,32,4,128]{3,1,2,0:T(8,128)(2,1)S(1)} %fusion.31), channel_id=1, replica_groups=mesh['row'=32,'chan'=16] {'chan'}, dimensions={1}, use_global_device_ids=true | all-gather | bytes 557056 | tf_op jit(solution)/shard_map/all_gather | solution.py:53
  118.4 1.9 collective-permute-start.2
  120.4 3.6 collective-permute-start.3
  124.2 1.5 fusion.30
  125.7 2.1 fusion.29
  129.8 2.9 copy.34
  132.9 3.3 collective-permute-done.3
  137.8 1.6 fusion.49
  139.4 1.4 fusion.47
  140.9 1.6 fusion.45
  142.5 1.4 fusion.43
  144.1 0.8 constant_dynamic-update-slice_fusion.4
  146.6 1.5 fusion.80
  148.1 2.1 fusion.77
  151.1 2.1 fusion.64
  153.9 3.3 copy.37
  157.2 5.9 reshape.1983
  165.2 0.8 copy.35
  166.0 340.4 %all-reduce.8.cloned.1.call-done = f32[3,3,32,512]{2,1,0,3:T(4,128)} async-done(((f32[3,3,32,512]{2,1,0,3:T(4,128)}), f32[3,3,32,512]{2,1,0,3:T(4,128)}) %all-reduce.8.cloned.1.call-update) | async-done | bytes 589840
  506.4 0.9 constant_dynamic-slice_fusion
  507.9 115.9 %reduce-scatter.4.cloned.1.call-done = f32[16,256]{1,0:T(8,128)} async-done(((f32[512,256]{1,0:T(8,128)}), f32[16,256]{1,0:T(8,128)}) %reduce-scatter.4.cloned.1.call-update) | async-done | bytes 16400
  623.8 0.8 reshape.1984
  (108 shorter events, 16.4 us)
Async XLA Ops:
  7.2 499.2 %all-reduce.8.cloned.1.call-start = ((), (), s32[]{:S(2)}) async-start(), calls=%async_computation.2 | async-start | bytes 6291456
  54.5 21.0 %copy-start.1 = (bf16[3,3,32,512]{3,2,1,0:T(8,128)(2,1)S(1)}, bf16[3,3,32,512]{3,2,1,0:T(8,128)(2,1)}, u32[]{:S(2)}) copy-start(bf16[3,3,32,512]{3,2,1,0:T(8,128)(2,1)} %param.91) | copy-start | bytes 884740
  54.5 20.2 %collective-permute-start = (bf16[1,512,1,128]{3,1,2,0:T(8,128)(2,1)S(1)}, bf16[1,512,1,128]{3,1,2,0:T(8,128)(2,1)S(1)}, u32[]{:S(2)}, u32[]{:S(2)}) collective-permute-start(bf16[1,512,1,128]{3,1,2,0:T(8,128)(2,1)S(1)} %get-tuple-element.508), channel_id=1, source_target_pairs={{0,16},{16,32},{32,48},{48,64},{64,80},{80,96},{96,112},{112,128},... | collective-permute-start | bytes 393224 | tf_op jit(solution)/shard_map/ppermute | solution.py:14
  56.5 18.1 %collective-permute-start.1 = (bf16[1,512,1,128]{3,1,2,0:T(8,128)(2,1)S(1)}, bf16[1,512,1,128]{3,1,2,0:T(8,128)(2,1)S(1)}, u32[]{:S(2)}, u32[]{:S(2)}) collective-permute-start(bf16[1,512,1,128]{3,1,2,0:T(8,128)(2,1)S(1)} %get-tuple-element.509), channel_id=1, source_target_pairs={{16,0},{32,16},{48,32},{64,48},{80,64},{96,80},{112,96},{128,112},... | collective-permute-start | bytes 393224 | tf_op jit(solution)/shard_map/ppermute | solution.py:17
  69.3 48.9 %copy-start.8 = (bf16[1,16,4,128]{3,2,1,0:T(4,128)(2,1)}, bf16[1,16,4,128]{3,2,1,0:T(4,128)(2,1)S(1)}, u32[]{:S(2)}) copy-start(bf16[1,16,4,128]{3,2,1,0:T(4,128)(2,1)S(1)} %slice.1582) | copy-start | bytes 49156
  74.7 1.3 copy-start
  77.3 40.6 %copy-start.2 = (bf16[4,4,16,512]{3,2,1,0:T(8,128)(2,1)S(1)}, bf16[4,4,16,512]{3,2,1,0:T(8,128)(2,1)}, u32[]{:S(2)}) copy-start(bf16[4,4,16,512]{3,2,1,0:T(8,128)(2,1)} %param.90) | copy-start | bytes 786436
  118.4 14.5 %collective-permute-start.2 = (bf16[1,512,1,128]{3,1,2,0:T(8,128)(2,1)S(1)}, bf16[1,512,1,128]{3,1,2,0:T(8,128)(2,1)S(1)}, u32[]{:S(2)}, u32[]{:S(2)}) collective-permute-start(bf16[1,512,1,128]{3,1,2,0:T(8,128)(2,1)S(1)} %get-tuple-element.506), channel_id=1, source_target_pairs={{0,16},{16,32},{32,48},{48,64},{64,80},{80,96},{96,112},{112,128},... | collective-permute-start | bytes 393224 | tf_op jit(solution)/shard_map/ppermute | solution.py:14
  120.4 15.9 %collective-permute-start.3 = (bf16[1,512,1,128]{3,1,2,0:T(8,128)(2,1)S(1)}, bf16[1,512,1,128]{3,1,2,0:T(8,128)(2,1)S(1)}, u32[]{:S(2)}, u32[]{:S(2)}) collective-permute-start(bf16[1,512,1,128]{3,1,2,0:T(8,128)(2,1)S(1)} %get-tuple-element.507), channel_id=1, source_target_pairs={{16,0},{32,16},{48,32},{64,48},{80,64},{96,80},{112,96},{128,112},... | collective-permute-start | bytes 393224 | tf_op jit(solution)/shard_map/ppermute | solution.py:17
  132.7 4.4 copy-start.9
  132.7 491.1 %reduce-scatter.4.cloned.1.call-start = ((), (), s32[]{:S(2)}) async-start(), calls=%async_computation.1 | async-start | bytes 540672
  136.2 14.9 %copy-start.3 = (bf16[1,512,1,128]{3,1,2,0:T(8,128)(2,1)}, bf16[1,512,1,128]{3,1,2,0:T(8,128)(2,1)S(1)}, u32[]{:S(2)}) copy-start(bf16[1,512,1,128]{3,1,2,0:T(8,128)(2,1)S(1)} %collective-permute-done.3) | copy-start | bytes 393220
  143.9 1.5 copy-start.7
  145.4 1.2 copy-start.6
  157.2 5.9 copy-start.5
  163.1 0.9 copy-start.4
Sparse Core Ops, SparseCore 0:
  132.8 373.5 all-reduce.7
  511.3 112.4 reduce-scatter.3
where the time goes:
time: 635 us; the launch traced here: 632 us
  waiting for transfers between devices  460 us (72%)
  blocking collectives  86.3 us (14%)
  local copies, waits for them, and re-layouts  30.2 us (5%)
  matrix products  26.4 us (4%)
  between operations  15 us (2%)
  starting transfers between devices  11.5 us (2%)
    unnamed x4, waiting for transfers between devices  456 us
    all_gather x1, blocking collectives, body(): gathered = lax.all_gather(cotangent, 'chan', axis=1, tiled=True)  46.5 us
    all_gather x1, blocking collectives, body(): gathered_hidden = lax.all_gather(grad_hidden, 'chan', axis=1, tiled=True)  39.9 us
    unnamed x29, local copies, waits for them, and re-layouts  15.5 us
  transfers between devices with their start and end apart: 6, of which 3 were waited for; matrix products, arithmetic and copies ran while one was open for 8% of the time, Pallas kernels for 0%

commit v1 on v0

v1 whole, which is shorter than its diff:
```python
import functools
import math

import jax
import jax.numpy as jnp
from jax import lax
from jax.experimental import pallas as pl
from jax.experimental.pallas import tpu as pltpu
from jax.sharding import PartitionSpec as P

MESH = pl.DeviceIdType.MESH
BF16 = jnp.bfloat16
F32 = jnp.float32
ROWS = 32
N_CHAN = 16
HID = 32
CIN = 16
OW = 128
OUT_ROWS = 4
PIX = OUT_ROWS * OW
C = 512


def iota2(shape, dim):
    return lax.broadcasted_iota(jnp.int32, shape, dim)


def one_hot(shape, want):
    left, right = want(iota2(shape, 0), iota2(shape, 1))
    return jnp.where(left == right, 1.0, 0.0).astype(BF16)


def mm(a, b):
    return jnp.dot(a, b, preferred_element_type=F32)


def mm_nt(a, b):
    return lax.dot_general(a, b, (((1,), (1,)), ((), ())), preferred_element_type=F32)


def shift_right(x):
    lane = iota2(x.shape, 1)
    return jnp.where(lane == 0, 0.0, pltpu.roll(x, 1, axis=1))


def shift_left(x):
    lane = iota2(x.shape, 1)
    width = x.shape[1]
    return jnp.where(lane == width - 1, 0.0, pltpu.roll(x, width - 1, axis=1))


def square_cols(g):
    return g[HID : 2 * HID] + shift_right(g[2 * HID :]) + shift_left(g[:HID])


def strided_cols(g):
    t = [g[k * CIN : (k + 1) * CIN] for k in range(4)]
    return t[1] + shift_right(t[3]), t[2] + shift_left(t[0])


def kernel(
    feat_hbm, pre_hbm, cot_hbm, ws_hbm, wq_hbm,
    gf_hbm, gs_hbm, gq_hbm,
    feat_v, pre_v, cot_v, ws_v, wq_v,
    cotg, hidg, pre_t, ax, fx, a_sel, f_sel, ab, fb,
    ga_send, ga_recv, gf_send, gf_recv,
    q_own, q1, q1r, q2, q2r, q3, q3r,
    s_own, s1, s1r, s2, s2r, s3, s3r,
    gf_v, gs_v, gq_v,
    local_sem, gat_send, gat_recv, halo_ssem, halo_rsem, rs_ssem, rs_rsem,
):
    r, h = lax.axis_index("row"), lax.axis_index("chan")
    zh, y, core = r // 8, (r // 2) % 4, r % 2
    z, x = h // 4, h % 4
    up, down = ((r + ROWS - 1) % ROWS, h), ((r + 1) % ROWS, h)
    z_ids = [z + 1 - 2 * (z % 2), (z + 2) % 4, 3 - z]
    x_ids = [(x + 1) % 4, (x + 3) % 4, (x + 2) % 4]
    y_ids = [(y + 1) % 4, (y + 3) % 4, (y + 2) % 4]
    zh_ids = [(zh + 1) % 4, (zh + 3) % 4, (zh + 2) % 4]
    core_peer = (zh * 8 + y * 2 + (1 - core), h)
    y_peers = [(zh * 8 + p * 2 + core, h) for p in y_ids]
    zh_peers = [(p * 8 + y * 2 + core, h) for p in zh_ids]
    z_peers = [(r, p * 4 + x) for p in z_ids]
    x_peers = [(r, z * 4 + p) for p in x_ids]

    loads = [
        pltpu.make_async_copy(src, dst, local_sem.at[k])
        for k, (src, dst) in enumerate(
            [(cot_hbm, cot_v), (pre_hbm, pre_v), (feat_hbm, feat_v), (wq_hbm, wq_v), (ws_hbm, ws_v)]
        )
    ]
    for load in loads:
        load.start()
    partners = [core_peer, *y_peers, *zh_peers, *z_peers, *x_peers, up, down]
    barrier = pltpu.get_barrier_semaphore()
    for peer in partners:
        pl.semaphore_signal(barrier, inc=1, device_id=peer, device_id_type=MESH)

    sent = []

    def copy(src, dst, ssem, rsem, dev):
        return pltpu.make_async_remote_copy(
            src_ref=src, dst_ref=dst, send_sem=ssem, recv_sem=rsem, device_id=dev, device_id_type=MESH
        )

    def send(src, dst, ssem, rsem, dev):
        c = copy(src, dst, ssem, rsem, dev)
        c.start()
        sent.append(c)
        return c

    by_row = one_hot((128, 128), lambda i, j: (j, (i % HID) * OUT_ROWS + i // HID))
    loads[0].wait()
    cot_t = mm(by_row, cot_v[...]).astype(BF16)
    mine = pl.ds(pl.multiple_of(h * HID, HID), HID)
    for a in range(OUT_ROWS):
        cotg[mine, a * OW : (a + 1) * OW] = cot_t[a * HID : (a + 1) * HID]
    pl.semaphore_wait(barrier, len(partners))

    def block(buf, b):
        return buf.at[pl.ds(pl.multiple_of(b * HID, HID), HID)]

    def gather_start(buf, n):
        count = [0]

        def put(b, dev):
            ref = block(buf, b)
            send(ref, ref, gat_send.at[n, count[0]], gat_recv.at[n, b], dev)
            count[0] += 1

        def take(b):
            ref = block(buf, b)
            copy(ref, ref, gat_send.at[n, 0], gat_recv.at[n, b], (r, h)).wait_recv()

        for dev in z_peers:
            put(h, dev)
        for dev in x_peers:
            put(h, dev)
        return put, take

    def gather_forward(put, take):
        for p in z_ids:
            take(p * 4 + x)
            for dev in x_peers:
                put(p * 4 + x, dev)

    def gather_finish(take):
        for zz in [z, *z_ids]:
            for xx in x_ids:
                take(zz * 4 + xx)

    put, take = gather_start(cotg, 0)

    loads[1].wait()
    pre_rows = mm(by_row, pre_v[...]).astype(BF16)
    pre_t[...] = pre_rows
    ax[HID : HID + 128] = jnp.maximum(pre_rows, 0)
    halo = [
        send(ax.at[pl.ds(HID, HID)], ax.at[pl.ds(HID + 128, HID)], halo_ssem.at[0], halo_rsem.at[0], up),
        send(ax.at[pl.ds(128, HID)], ax.at[pl.ds(0, HID)], halo_ssem.at[1], halo_rsem.at[1], down),
    ]
    loads[2].wait()
    f_by_row = one_hot((128, 128), lambda i, j: (j, (i % CIN) * 8 + i // CIN))
    fx[CIN : CIN + 128] = mm(f_by_row, feat_v[...]).astype(BF16)
    halo += [
        send(fx.at[pl.ds(CIN, CIN)], fx.at[pl.ds(CIN + 128, CIN)], halo_ssem.at[2], halo_rsem.at[2], up),
        send(fx.at[pl.ds(128, CIN)], fx.at[pl.ds(0, CIN)], halo_ssem.at[3], halo_rsem.at[3], down),
    ]
    gather_forward(put, take)

    for c in halo:
        c.wait_recv()
    first, last = r == 0, r == ROWS - 1
    shifts = one_hot((OW, 3 * OW), lambda i, j: (i, j % OW + j // OW - 1))
    a_sel[...] = mm(ax[...], shifts).astype(BF16)
    strides = one_hot((2 * OW, 4 * OW), lambda i, j: (i, 2 * (j % OW) + j // OW - 1))
    f_sel[...] = mm(fx[...], strides).astype(BF16)
    a_sel[:HID] = jnp.where(first, 0.0, a_sel[:HID].astype(F32)).astype(BF16)
    a_sel[HID + 128 :] = jnp.where(last, 0.0, a_sel[HID + 128 :].astype(F32)).astype(BF16)
    f_sel[:CIN] = jnp.where(first, 0.0, f_sel[:CIN].astype(F32)).astype(BF16)
    f_sel[CIN + 128 :] = jnp.where(last, 0.0, f_sel[CIN + 128 :].astype(F32)).astype(BF16)
    for ky in range(3):
        for kx in range(3):
            t = ky * 3 + kx
            for p in range(OUT_ROWS):
                ab[t * HID : (t + 1) * HID, p * OW : (p + 1) * OW] = a_sel[
                    (p + ky) * HID : (p + ky + 1) * HID, kx * OW : (kx + 1) * OW
                ]
    for ky in range(4):
        for kx in range(4):
            t = ky * 4 + kx
            for p in range(OUT_ROWS):
                fb[t * CIN : (t + 1) * CIN, p * OW : (p + 1) * OW] = f_sel[
                    (2 * p + ky) * CIN : (2 * p + ky + 1) * CIN, kx * OW : (kx + 1) * OW
                ]
    loads[3].wait()
    loads[4].wait()
    gather_finish(take)

    ga_send[0] = square_cols(mm(wq_v[: 3 * HID], cotg[:, :OW]))
    ga_send[1] = square_cols(mm(wq_v[6 * HID :], cotg[:, PIX - OW :]))
    ga_halo = [
        send(ga_send.at[0], ga_recv.at[0], halo_ssem.at[4], halo_rsem.at[4], up),
        send(ga_send.at[1], ga_recv.at[1], halo_ssem.at[5], halo_rsem.at[5], down),
    ]
    g = mm(wq_v[...], cotg[...])
    rows = [None] * OUT_ROWS
    for ky in range(3):
        for a in range(OUT_ROWS):
            p = a + ky - 1
            if 0 <= p < OUT_ROWS:
                term = square_cols(g[ky * 3 * HID : (ky + 1) * 3 * HID, a * OW : (a + 1) * OW])
                rows[p] = term if rows[p] is None else rows[p] + term
    for c in ga_halo:
        c.wait_recv()
    rows[0] = rows[0] + jnp.where(first, 0.0, ga_recv[1])
    rows[3] = rows[3] + jnp.where(last, 0.0, ga_recv[0])
    for p in range(OUT_ROWS):
        gate = pre_t[p * HID : (p + 1) * HID].astype(F32) > 0
        hidg[mine, p * OW : (p + 1) * OW] = jnp.where(gate, rows[p], 0.0).astype(BF16)
    put, take = gather_start(hidg, 1)

    scale = 1.0 / math.sqrt(128 * 128)

    def spread(full, own, wire):
        for zz in range(4):
            for yy in range(4):
                for cc in range(2):
                    src = (zz * 8 + yy * 2 + cc) * 16
                    dst = (cc * 16 + yy * 4 + zz) * 16
                    part = full[src : src + 16]
                    own[dst : dst + 16] = part
                    wire[dst : dst + 16] = part.astype(BF16)

    def step_core(wire, got, n):
        part = wire.at[pl.ds(pl.multiple_of((1 - core) * 256, 256), 256)]
        return [send(part, got, rs_ssem.at[n, 0], rs_rsem.at[n, 0], core_peer)]

    def step_y(cs, own, got, wire, got2, n):
        for c in cs:
            c.wait_recv()
        half = pl.ds(pl.multiple_of(core * 256, 256), 256)
        total = own[half] + got[...].astype(F32)
        own[:256] = total
        wire[...] = total.astype(BF16)
        return [
            send(wire.at[pl.ds(pl.multiple_of(p * 64, 64), 64)], got2.at[k], rs_ssem.at[n, 1 + k], rs_rsem.at[n, 1 + k], dev)
            for k, (p, dev) in enumerate(zip(y_ids, y_peers))
        ]

    def step_z(cs, own, got2, wire, got3, n):
        for c in cs:
            c.wait_recv()
        total = own[pl.ds(pl.multiple_of(y * 64, 64), 64)]
        for k in range(3):
            total = total + got2[k].astype(F32)
        own[:64] = total
        wire[...] = total.astype(BF16)
        return [
            send(wire.at[pl.ds(pl.multiple_of(p * 16, 16), 16)], got3.at[k], rs_ssem.at[n, 4 + k], rs_rsem.at[n, 4 + k], dev)
            for k, (p, dev) in enumerate(zip(zh_ids, zh_peers))
        ]

    def step_end(cs, own, got3):
        for c in cs:
            c.wait_recv()
        total = own[pl.ds(pl.multiple_of(zh * 16, 16), 16)]
        for k in range(3):
            total = total + got3[k].astype(F32)
        return total * scale

    spread(mm_nt(cotg[...], ab[...]), q_own, q1)
    q_cs = step_core(q1, q1r, 0)
    gather_forward(put, take)
    q_cs = step_y(q_cs, q_own, q1r, q2, q2r, 0)
    gather_finish(take)

    spread(mm_nt(hidg[...], fb[...]), s_own, s1)
    s_cs = step_core(s1, s1r, 1)
    for n, (lo, col) in enumerate(((0, 0), (12 * CIN, PIX - OW))):
        a, b = strided_cols(mm(ws_v[lo : lo + 4 * CIN], hidg[:, col : col + OW]))
        gf_send[n, :CIN] = a
        gf_send[n, CIN:] = b
    gf_halo = [
        send(gf_send.at[0], gf_recv.at[0], halo_ssem.at[6], halo_rsem.at[6], up),
        send(gf_send.at[1], gf_recv.at[1], halo_ssem.at[7], halo_rsem.at[7], down),
    ]
    g = mm(ws_v[...], hidg[...])
    s_cs = step_y(s_cs, s_own, s1r, s2, s2r, 1)
    q_cs = step_z(q_cs, q_own, q2r, q3, q3r, 0)

    def taps(ky, i):
        return strided_cols(g[ky * 4 * CIN : (ky + 1) * 4 * CIN, i * OW : (i + 1) * OW])

    parts = []
    for f in range(8):
        u = f // 2
        if f % 2 == 0:
            near, far = taps(1, u), (taps(3, u - 1) if u else None)
        else:
            near, far = taps(2, u), (taps(0, u + 1) if u < 3 else None)
        parts.append((near, far))
    for c in gf_halo:
        c.wait_recv()
    above = jnp.where(first, 0.0, gf_recv[1])
    below = jnp.where(last, 0.0, gf_recv[0])
    lines = []
    for f, (near, far) in enumerate(parts):
        if far is None:
            edge = above if f == 0 else below
            far = (edge[:CIN], edge[CIN:])
        lines.append(jnp.concatenate([near[0] + far[0], near[1] + far[1]], axis=1).astype(BF16))
    phased = jnp.concatenate(lines, axis=0)
    weave = one_hot((2 * OW, 2 * OW), lambda i, j: (j, 2 * (i % OW) + i // OW))
    by_channel = one_hot((128, 128), lambda i, j: (j, (i % 8) * CIN + i // 8))
    woven = mm(phased, weave).astype(BF16)
    gf_v[...] = mm(by_channel, woven).astype(BF16)
    out_gf = pltpu.make_async_copy(gf_v, gf_hbm, local_sem.at[5])
    out_gf.start()

    s_cs = step_z(s_cs, s_own, s2r, s3, s3r, 1)
    gq = step_end(q_cs, q_own, q3r)
    for t in range(9):
        gq_v[t] = gq[:, t * HID : (t + 1) * HID]
    out_gq = pltpu.make_async_copy(gq_v, gq_hbm, local_sem.at[6])
    out_gq.start()
    gs_v[...] = step_end(s_cs, s_own, s3r)
    out_gs = pltpu.make_async_copy(gs_v, gs_hbm, local_sem.at[7])
    out_gs.start()
    for c in sent:
        c.wait_send()
    out_gf.wait()
    out_gq.wait()
    out_gs.wait()


def body(features, pre_act, cotangent, w_strided, w_square):
    nq, ns = 9 * HID, 16 * CIN
    any_spec = pl.BlockSpec(memory_space=pl.ANY)
    vm = pltpu.VMEM
    scratch = [
        vm((128, 256), BF16), vm((128, 128), BF16), vm((128, 128), BF16), vm((ns, C), BF16), vm((nq, C), BF16),
        vm((C, PIX), BF16), vm((C, PIX), BF16), vm((128, 128), BF16), vm((192, 128), BF16), vm((160, 256), BF16),
        vm((192, 384), BF16), vm((160, 512), BF16), vm((nq, PIX), BF16), vm((ns, PIX), BF16),
        vm((2, 32, 128), F32), vm((2, 32, 128), F32), vm((2, 32, 128), F32), vm((2, 32, 128), F32),
    ]
    for n in (nq, ns):
        scratch += [
            vm((C, n), F32), vm((C, n), BF16), vm((256, n), BF16), vm((256, n), BF16), vm((3, 64, n), BF16),
            vm((64, n), BF16), vm((3, 16, n), BF16),
        ]
    scratch += [vm((128, 256), BF16), vm((16, ns), F32), vm((9, 16, HID), F32)]
    dma = pltpu.SemaphoreType.DMA
    scratch += [dma((8,)), dma((2, 15)), dma((2, N_CHAN)), dma((8,)), dma((8,)), dma((2, 7)), dma((2, 7))]
    gf, gs, gq = pl.pallas_call(
        kernel,
        out_shape=(
            jax.ShapeDtypeStruct((128, 256), BF16),
            jax.ShapeDtypeStruct((16, ns), F32),
            jax.ShapeDtypeStruct((9, 16, HID), F32),
        ),
        in_specs=[any_spec] * 5,
        out_specs=[any_spec] * 3,
        scratch_shapes=scratch,
        compiler_params=pltpu.CompilerParams(
            collective_id=0, has_side_effects=True, vmem_limit_bytes=40 * 2**20
        ),
        name="backward",
    )(
        features.reshape(128, 256),
        pre_act.reshape(128, 128),
        cotangent.reshape(128, 128),
        w_strided.reshape(ns, C),
        w_square.reshape(nq, C),
    )
    grad_features = gf.reshape(features.shape)
    strided = jnp.transpose(gs.reshape(16, 4, 4, CIN), (1, 2, 3, 0))
    square = jnp.transpose(gq.reshape(3, 3, 16, HID), (0, 1, 3, 2))
    return grad_features, strided, square


def solution(mesh):
    in_specs = (
        P(None, "chan", "row", None),
        P(None, "chan", "row", None),
        P(None, "chan", "row", None),
        P(None, None, "chan", None),
        P(None, None, "chan", None),
    )
    out_specs = (
        P(None, "chan", "row", None),
        P(None, None, "chan", "row"),
        P(None, None, "chan", "row"),
    )
    return jax.shard_map(body, mesh=mesh, in_specs=in_specs, out_specs=out_specs, check_vma=False)
```

time: 635 us -> 58.1 us (0.09)
  the two profiles are of different devices: /device:TPU:24 before, /device:TPU:32 now
where the time goes in v1:
time: 58.1 us; the launch traced here: 57.7 us
  Pallas kernels  50.8 us (87%)
  local copies, waits for them, and re-layouts  6.27 us (11%)
  between operations  0.65 us (1%)
    pallas_call x1, Pallas kernels, body(): pl.pallas_call(kernel, out_shape=(jax.ShapeDtypeStruct((128, 256), BF16),...  50.8 us
    unnamed x12, local copies, waits for them, and re-layouts  5.52 us

profile of v1, /device:TPU:32, one launch (start us, length us, event | category | flops | bytes accessed | tf_op | source)
XLA Modules:
  0.0 57.7 jit_solution(5123936236122513803)
XLA Ops:
  0.6 0.0 copy-start
  0.6 1.0 %copy-done = bf16[3,3,32,512]{3,2,1,0:T(8,128)(2,1)S(1)} copy-done((bf16[3,3,32,512]{3,2,1,0:T(8,128)(2,1)S(1)}, bf16[3,3,32,512]{3,2,1,0:T(8,128)(2,1)}, u32[]{:S(2)}) %copy-start) | copy-done | bytes 294936
  1.6 0.0 copy-start.1
  1.6 0.9 %copy-done.1 = bf16[4,4,16,512]{3,2,1,0:T(8,128)(2,1)S(1)} copy-done((bf16[4,4,16,512]{3,2,1,0:T(8,128)(2,1)S(1)}, bf16[4,4,16,512]{3,2,1,0:T(8,128)(2,1)}, u32[]{:S(2)}) %copy-start.1) | copy-done | bytes 262168
  2.5 0.0 copy-start.2
  2.5 0.8 %copy-done.2 = bf16[1,16,8,256]{3,2,1,0:T(8,128)(2,1)S(1)} copy-done((bf16[1,16,8,256]{3,2,1,0:T(8,128)(2,1)S(1)}, bf16[1,16,8,256]{3,2,1,0:T(8,128)(2,1)}, u32[]{:S(2)}) %copy-start.2) | copy-done | bytes 65560
  3.4 0.0 copy-start.3
  3.4 0.8 %copy-done.3 = bf16[1,32,4,128]{3,2,1,0:T(4,128)(2,1)S(1)} copy-done((bf16[1,32,4,128]{3,2,1,0:T(4,128)(2,1)S(1)}, bf16[1,32,4,128]{3,2,1,0:T(4,128)(2,1)}, u32[]{:S(2)}) %copy-start.3) | copy-done | bytes 32792
  4.1 0.0 copy-start.4
  4.1 0.8 %copy-done.4 = bf16[1,32,4,128]{3,2,1,0:T(4,128)(2,1)S(1)} copy-done((bf16[1,32,4,128]{3,2,1,0:T(4,128)(2,1)S(1)}, bf16[1,32,4,128]{3,2,1,0:T(4,128)(2,1)}, u32[]{:S(2)}) %copy-start.4) | copy-done | bytes 32792
  4.9 50.8 %backward.1 = (bf16[128,256]{1,0:T(8,128)(2,1)S(1)}, f32[16,256]{1,0:T(8,128)S(1)}, f32[9,16,32]{2,1,0:T(8,128)S(1)}) custom-call(bf16[128,256]{1,0:T(8,128)(2,1)S(1)} %bitcast.16, bf16[128,128]{1,0:T(8,128)(2,1)S(1)} %bitcast.17, bf16[128,128]{1,0:T(8,128)(2,1)S(1)} %bitcast.18, bf16[256,512]{1,0:T(8,128)(2,1)S(1)} %bitcast.13, bf16[288,512]{1,0:T(8,128)(2,1)S(1)} %bitcast.12), custom_call_target="tpu_custom_call" | custom-call | tf_op jit(solution)/shard_map/backward/pallas_call | solution.py:355
  55.7 0.8 %copy.9 = f32[16,256]{0,1:T(8,128)} copy(f32[16,256]{1,0:T(8,128)S(1)} %get-tuple-element.7) | data formatting | bytes 32768 | tf_op jit(solution)/shard_map/reshape | solution.py:377
  56.4 0.6 %copy.12 = bf16[1,16,8,256]{3,2,1,0:T(8,128)(2,1)} copy(bf16[1,16,8,256]{3,2,1,0:T(8,128)(2,1)S(1)} %bitcast.15) | data formatting | bytes 131072
  57.1 0.6 %copy.13 = f32[3,3,32,16]{2,3,1,0:T(8,128)} copy(f32[3,3,32,16]{2,3,1,0:T(8,128)S(1)} %bitcast.14) | data formatting | bytes 36864
Async XLA Ops:
  0.6 1.0 %copy-start = (bf16[3,3,32,512]{3,2,1,0:T(8,128)(2,1)S(1)}, bf16[3,3,32,512]{3,2,1,0:T(8,128)(2,1)}, u32[]{:S(2)}) copy-start(bf16[3,3,32,512]{3,2,1,0:T(8,128)(2,1)} %param.9) | copy-start | bytes 884740
  1.6 0.9 %copy-start.1 = (bf16[4,4,16,512]{3,2,1,0:T(8,128)(2,1)S(1)}, bf16[4,4,16,512]{3,2,1,0:T(8,128)(2,1)}, u32[]{:S(2)}) copy-start(bf16[4,4,16,512]{3,2,1,0:T(8,128)(2,1)} %param.8) | copy-start | bytes 786436
  2.5 0.8 %copy-start.2 = (bf16[1,16,8,256]{3,2,1,0:T(8,128)(2,1)S(1)}, bf16[1,16,8,256]{3,2,1,0:T(8,128)(2,1)}, u32[]{:S(2)}) copy-start(bf16[1,16,8,256]{3,2,1,0:T(8,128)(2,1)} %param.5) | copy-start | bytes 196612
  3.4 0.8 %copy-start.3 = (bf16[1,32,4,128]{3,2,1,0:T(4,128)(2,1)S(1)}, bf16[1,32,4,128]{3,2,1,0:T(4,128)(2,1)}, u32[]{:S(2)}) copy-start(bf16[1,32,4,128]{3,2,1,0:T(4,128)(2,1)} %param.6) | copy-start | bytes 98308
  4.1 0.8 %copy-start.4 = (bf16[1,32,4,128]{3,2,1,0:T(4,128)(2,1)S(1)}, bf16[1,32,4,128]{3,2,1,0:T(4,128)(2,1)}, u32[]{:S(2)}) copy-start(bf16[1,32,4,128]{3,2,1,0:T(4,128)(2,1)} %param.7) | copy-start | bytes 98308

commit v2 on v1

--- a/solution.py
+++ b/solution.py
@@ -62,12 +62,12 @@
     feat_hbm, pre_hbm, cot_hbm, ws_hbm, wq_hbm,
     gf_hbm, gs_hbm, gq_hbm,
     feat_v, pre_v, cot_v, ws_v, wq_v,
-    cotg, hidg, pre_t, ax, fx, a_sel, f_sel, ab, fb,
-    ga_send, ga_recv, gf_send, gf_recv,
+    cotg, hidg, cot_t, edge, pre_t, ax, fx, a_sel, ab, fb,
+    gf_send, gf_recv,
     q_own, q1, q1r, q2, q2r, q3, q3r,
     s_own, s1, s1r, s2, s2r, s3, s3r,
     gf_v, gs_v, gq_v,
-    local_sem, gat_send, gat_recv, halo_ssem, halo_rsem, rs_ssem, rs_rsem,
+    local_sem, gat_send, gat_recv, halo_ssem, halo_rsem, edge_ssem, edge_rsem, fx_ssem, fx_rsem, rs_ssem, rs_rsem,
 ):
     r, h = lax.axis_index("row"), lax.axis_index("chan")
     zh, y, core = r // 8, (r // 2) % 4, r % 2
@@ -82,6 +82,11 @@
     zh_peers = [(p * 8 + y * 2 + core, h) for p in zh_ids]
     z_peers = [(r, p * 4 + x) for p in z_ids]
     x_peers = [(r, z * 4 + p) for p in x_ids]
+    owner_ids = [(z + k) % 4 for k in range(4)]
+    owners = [(z * 8 + y * 2 + core, p * 4 + x) for p in owner_ids]
+    giver_ids = [(zh + k) % 4 for k in range(4)]
+    givers = [(p * 8 + y * 2 + core, zh * 4 + x) for p in giver_ids]
+    keeps = zh == z
 
     loads = [
         pltpu.make_async_copy(src, dst, local_sem.at[k])
@@ -91,10 +96,16 @@
     ]
     for load in loads:
         load.start()
-    partners = [core_peer, *y_peers, *zh_peers, *z_peers, *x_peers, up, down]
+    edges = [((r + d) % ROWS, p * 4 + x) for d in (ROWS - 1, 1) for p in range(4)]
+    next_plane = [(r, z_ids[0] * 4 + p) for p in x_ids]
+    partners = [core_peer, *y_peers, *zh_peers, *z_peers, *x_peers, *next_plane, *edges, *givers[1:]]
     barrier = pltpu.get_barrier_semaphore()
     for peer in partners:
         pl.semaphore_signal(barrier, inc=1, device_id=peer, device_id_type=MESH)
+
+    @pl.when(jnp.logical_not(keeps))
+    def _():
+        pl.semaphore_signal(barrier, inc=1, device_id=givers[0], device_id_type=MESH)
 
     sent = []
 
@@ -111,11 +122,11 @@
 
     by_row = one_hot((128, 128), lambda i, j: (j, (i % HID) * OUT_ROWS + i // HID))
     loads[0].wait()
-    cot_t = mm(by_row, cot_v[...]).astype(BF16)
+    cot_t[...] = mm(by_row, cot_v[...]).astype(BF16)
     mine = pl.ds(pl.multiple_of(h * HID, HID), HID)
     for a in range(OUT_ROWS):
         cotg[mine, a * OW : (a + 1) * OW] = cot_t[a * HID : (a + 1) * HID]
-    pl.semaphore_wait(barrier, len(partners))
+    pl.semaphore_wait(barrier, len(partners) + jnp.where(keeps, 0, 1))
 
     def block(buf, b):
         return buf.at[pl.ds(pl.multiple_of(b * HID, HID), HID)]
@@ -132,22 +143,30 @@
             ref = block(buf, b)
             copy(ref, ref, gat_send.at[n, 0], gat_recv.at[n, b], (r, h)).wait_recv()
 
-        for dev in z_peers:
-            put(h, dev)
-        for dev in x_peers:
+        firsts = z_peers[1:] + x_peers + [z_peers[0]] + next_plane if n == 0 else x_peers + z_peers[1:] + [z_peers[0]] + next_plane
+        for dev in firsts:
             put(h, dev)
         return put, take
 
     def gather_forward(put, take):
-        for p in z_ids:
+        for p in z_ids[1:]:
             take(p * 4 + x)
             for dev in x_peers:
                 put(p * 4 + x, dev)
 
     def gather_finish(take):
+        take(z_ids[0] * 4 + x)
         for zz in [z, *z_ids]:
             for xx in x_ids:
                 take(zz * 4 + xx)
+
+    for n, (d, lo, side) in enumerate(((ROWS - 1, 0, 1), (1, 96, 0))):
+        for k in range(4):
+            p = (z + k) % 4
+            send(
+                cot_t.at[pl.ds(lo, HID)], edge.at[h, pl.ds(side * HID, HID)], edge_ssem.at[n * 4 + k],
+                edge_rsem.at[h, side], ((r + d) % ROWS, p * 4 + x),
+            )
 
     put, take = gather_start(cotg, 0)
 
@@ -161,24 +180,37 @@
     ]
     loads[2].wait()
     f_by_row = one_hot((128, 128), lambda i, j: (j, (i % CIN) * 8 + i // CIN))
-    fx[CIN : CIN + 128] = mm(f_by_row, feat_v[...]).astype(BF16)
+    fx[z, CIN : CIN + 128] = mm(f_by_row, feat_v[...]).astype(BF16)
     halo += [
-        send(fx.at[pl.ds(CIN, CIN)], fx.at[pl.ds(CIN + 128, CIN)], halo_ssem.at[2], halo_rsem.at[2], up),
-        send(fx.at[pl.ds(128, CIN)], fx.at[pl.ds(0, CIN)], halo_ssem.at[3], halo_rsem.at[3], down),
+        send(fx.at[z, pl.ds(CIN, CIN)], fx.at[z, pl.ds(CIN + 128, CIN)], halo_ssem.at[2], halo_rsem.at[2], up),
+        send(fx.at[z, pl.ds(128, CIN)], fx.at[z, pl.ds(0, CIN)], halo_ssem.at[3], halo_rsem.at[3], down),
     ]
     gather_forward(put, take)
+    for k in range(4):
+        b = (z + k) % 4 * 4 + x
+        for side in range(2):
+            ref = edge.at[b, pl.ds(side * HID, HID)]
+            copy(ref, ref, edge_ssem.at[0], edge_rsem.at[b, side], (r, h)).wait_recv()
+        for j, dev in enumerate(x_peers):
+            send(edge.at[b], edge.at[b], edge_ssem.at[8 + 3 * k + j], edge_rsem.at[b, 2], dev)
+
+    first, last = r == 0, r == ROWS - 1
+
+    def masked(flag, value):
+        return jnp.where(flag, 0.0, value.astype(F32)).astype(BF16)
 
     for c in halo:
         c.wait_recv()
-    first, last = r == 0, r == ROWS - 1
+    fxm = fx.at[z]
+    fxm[:CIN] = masked(first, fxm[:CIN])
+    fxm[CIN + 128 :] = masked(last, fxm[CIN + 128 :])
+    for k, (p, dev) in enumerate(zip(z_ids, z_peers)):
+        send(fxm, fxm, fx_ssem.at[k], fx_rsem.at[z], dev)
+
     shifts = one_hot((OW, 3 * OW), lambda i, j: (i, j % OW + j // OW - 1))
     a_sel[...] = mm(ax[...], shifts).astype(BF16)
-    strides = one_hot((2 * OW, 4 * OW), lambda i, j: (i, 2 * (j % OW) + j // OW - 1))
-    f_sel[...] = mm(fx[...], strides).astype(BF16)
-    a_sel[:HID] = jnp.where(first, 0.0, a_sel[:HID].astype(F32)).astype(BF16)
-    a_sel[HID + 128 :] = jnp.where(last, 0.0, a_sel[HID + 128 :].astype(F32)).astype(BF16)
-    f_sel[:CIN] = jnp.where(first, 0.0, f_sel[:CIN].astype(F32)).astype(BF16)
-    f_sel[CIN + 128 :] = jnp.where(last, 0.0, f_sel[CIN + 128 :].astype(F32)).astype(BF16)
+    a_sel[:HID] = masked(first, a_sel[:HID])
+    a_sel[HID + 128 :] = masked(last, a_sel[HID + 128 :])
     for ky in range(3):
         for kx in range(3):
             t = ky * 3 + kx
@@ -186,23 +218,10 @@
                 ab[t * HID : (t + 1) * HID, p * OW : (p + 1) * OW] = a_sel[
                     (p + ky) * HID : (p + ky + 1) * HID, kx * OW : (kx + 1) * OW
                 ]
-    for ky in range(4):
-        for kx in range(4):
-            t = ky * 4 + kx
-            for p in range(OUT_ROWS):
-                fb[t * CIN : (t + 1) * CIN, p * OW : (p + 1) * OW] = f_sel[
-                    (2 * p + ky) * CIN : (2 * p + ky + 1) * CIN, kx * OW : (kx + 1) * OW
-                ]
     loads[3].wait()
     loads[4].wait()
     gather_finish(take)
 
-    ga_send[0] = square_cols(mm(wq_v[: 3 * HID], cotg[:, :OW]))
-    ga_send[1] = square_cols(mm(wq_v[6 * HID :], cotg[:, PIX - OW :]))
-    ga_halo = [
-        send(ga_send.at[0], ga_recv.at[0], halo_ssem.at[4], halo_rsem.at[4], up),
-        send(ga_send.at[1], ga_recv.at[1], halo_ssem.at[5], halo_rsem.at[5], down),
-    ]
     g = mm(wq_v[...], cotg[...])
     rows = [None] * OUT_ROWS
     for ky in range(3):
@@ -211,10 +230,14 @@
             if 0 <= p < OUT_ROWS:
                 term = square_cols(g[ky * 3 * HID : (ky + 1) * 3 * HID, a * OW : (a + 1) * OW])
                 rows[p] = term if rows[p] is None else rows[p] + term
-    for c in ga_halo:
-        c.wait_recv()
-    rows[0] = rows[0] + jnp.where(first, 0.0, ga_recv[1])
-    rows[3] = rows[3] + jnp.where(last, 0.0, ga_recv[0])
+    for zz in range(4):
+        for xx in x_ids:
+            b = zz * 4 + xx
+            copy(edge.at[b], edge.at[b], edge_ssem.at[0], edge_rsem.at[b, 2], (r, h)).wait_recv()
+    above = square_cols(mm(wq_v[6 * HID :], edge[:, :HID].reshape(C, OW)))
+    below = square_cols(mm(wq_v[: 3 * HID], edge[:, HID:].reshape(C, OW)))
+    rows[0] = rows[0] + jnp.where(first, 0.0, above)
+    rows[3] = rows[3] + jnp.where(last, 0.0, below)
     for p in range(OUT_ROWS):
         gate = pre_t[p * HID : (p + 1) * HID].astype(F32) > 0
         hidg[mine, p * OW : (p + 1) * OW] = jnp.where(gate, rows[p], 0.0).astype(BF16)
@@ -271,12 +294,53 @@
 
     spread(mm_nt(cotg[...], ab[...]), q_own, q1)
     q_cs = step_core(q1, q1r, 0)
+
+    strides = one_hot((2 * OW, 4 * OW), lambda i, j: (i, 2 * (j % OW) + j // OW - 1))
+    for zz in range(4):
+
+        @pl.when(z != zz)
+        def _():
+            copy(fx.at[zz], fx.at[zz], fx_ssem.at[0], fx_rsem.at[zz], (r, h)).wait_recv()
+
+        f_sel = mm(fx[zz], strides).astype(BF16)
+        for ky in range(4):
+            for kx in range(4):
+                t = zz * 16 + ky * 4 + kx
+                for p in range(OUT_ROWS):
+                    fb[t * CIN : (t + 1) * CIN, p * OW : (p + 1) * OW] = f_sel[
+                        (2 * p + ky) * CIN : (2 * p + ky + 1) * CIN, kx * OW : (kx + 1) * OW
+                    ]
+
+    q_cs = step_y(q_cs, q_own, q1r, q2, q2r, 0)
+
+    for xx in x_ids:
+        take(z * 4 + xx)
+    full = mm_nt(hidg[pl.ds(pl.multiple_of(z * 128, 128), 128)], fb[...])
+    for yy in range(4):
+        for cc in range(2):
+            part = full[yy * 32 + cc * 16 : yy * 32 + cc * 16 + 16]
+            dst = cc * 64 + yy * 16
+            s_own[dst : dst + 16] = part
+            s1[dst : dst + 16] = part.astype(BF16)
+    s_core = send(
+        s1.at[pl.ds(pl.multiple_of((1 - core) * 64, 64), 64)], s1r, rs_ssem.at[1, 0], rs_rsem.at[1, 0], core_peer
+    )
     gather_forward(put, take)
-    q_cs = step_y(q_cs, q_own, q1r, q2, q2r, 0)
-    gather_finish(take)
-
-    spread(mm_nt(hidg[...], fb[...]), s_own, s1)
-    s_cs = step_core(s1, s1r, 1)
+
+    s_core.wait_recv()
+    total = s_own[pl.ds(pl.multiple_of(core * 64, 64), 64)] + s1r[...].astype(F32)
+    s_own[:64] = total
+    s2[...] = total.astype(BF16)
+    s_cs = [
+        send(s2.at[pl.ds(pl.multiple_of(p * 16, 16), 16)], s2r.at[k], rs_ssem.at[1, 1 + k], rs_rsem.at[1, 1 + k], dev)
+        for k, (p, dev) in enumerate(zip(y_ids, y_peers))
+    ]
+    q_cs = step_z(q_cs, q_own, q2r, q3, q3r, 0)
+    take(z_ids[0] * 4 + x)
+    for zz in z_ids:
+        for xx in x_ids:
+            take(zz * 4 + xx)
+
     for n, (lo, col) in enumerate(((0, 0), (12 * CIN, PIX - OW))):
         a, b = strided_cols(mm(ws_v[lo : lo + 4 * CIN], hidg[:, col : col + OW]))
         gf_send[n, :CIN] = a
@@ -286,8 +350,28 @@
         send(gf_send.at[1], gf_recv.at[1], halo_ssem.at[7], halo_rsem.at[7], down),
     ]
     g = mm(ws_v[...], hidg[...])
-    s_cs = step_y(s_cs, s_own, s1r, s2, s2r, 1)
-    q_cs = step_z(q_cs, q_own, q2r, q3, q3r, 0)
+    for c in s_cs:
+        c.wait_recv()
+    total = s_own[pl.ds(pl.multiple_of(y * 16, 16), 16)]
+    for k in range(3):
+        total = total + s2r[k].astype(F32)
+    for p in range(4):
+        s3[p] = total[:, p * 256 : (p + 1) * 256].astype(BF16)
+    last_sends = [
+        copy(s3.at[p], s3r.at[zh], rs_ssem.at[1, 4 + k], rs_rsem.at[1, 4 + zh], dev)
+        for k, (p, dev) in enumerate(zip(owner_ids, owners))
+    ]
+
+    @pl.when(keeps)
+    def _():
+        s3r[zh] = s3[z]
+
+    @pl.when(jnp.logical_not(keeps))
+    def _():
+        last_sends[0].start()
+
+    for c in last_sends[1:]:
+        c.start()
 
     def taps(ky, i):
         return strided_cols(g[ky * 4 * CIN : (ky + 1) * 4 * CIN, i * OW : (i + 1) * OW])
@@ -318,16 +402,32 @@
     out_gf = pltpu.make_async_copy(gf_v, gf_hbm, local_sem.at[5])
     out_gf.start()
 
-    s_cs = step_z(s_cs, s_own, s2r, s3, s3r, 1)
     gq = step_end(q_cs, q_own, q3r)
     for t in range(9):
         gq_v[t] = gq[:, t * HID : (t + 1) * HID]
     out_gq = pltpu.make_async_copy(gq_v, gq_hbm, local_sem.at[6])
     out_gq.start()
-    gs_v[...] = step_end(s_cs, s_own, s3r)
+    last_recvs = [
+        copy(s3.at[0], s3r.at[p], rs_ssem.at[1, 4], rs_rsem.at[1, 4 + p], dev) for p, dev in zip(giver_ids, givers)
+    ]
+
+    @pl.when(jnp.logical_not(keeps))
+    def _():
+        last_recvs[0].wait_recv()
+
+    for c in last_recvs[1:]:
+        c.wait_recv()
+    total = s3r[0].astype(F32)
+    for p in range(1, 4):
+        total = total + s3r[p].astype(F32)
+    gs_v[...] = total * scale
     out_gs = pltpu.make_async_copy(gs_v, gs_hbm, local_sem.at[7])
     out_gs.start()
-    for c in sent:
+    @pl.when(jnp.logical_not(keeps))
+    def _():
+        last_sends[0].wait_send()
+
+    for c in sent + last_sends[1:]:
         c.wait_send()
     out_gf.wait()
     out_gq.wait()
@@ -337,21 +437,22 @@
 def body(features, pre_act, cotangent, w_strided, w_square):
     nq, ns = 9 * HID, 16 * CIN
     any_spec = pl.BlockSpec(memory_space=pl.ANY)
+    hbm = lambda v: pltpu.with_memory_space_constraint(v, pltpu.HBM)
     vm = pltpu.VMEM
     scratch = [
         vm((128, 256), BF16), vm((128, 128), BF16), vm((128, 128), BF16), vm((ns, C), BF16), vm((nq, C), BF16),
-        vm((C, PIX), BF16), vm((C, PIX), BF16), vm((128, 128), BF16), vm((192, 128), BF16), vm((160, 256), BF16),
-        vm((192, 384), BF16), vm((160, 512), BF16), vm((nq, PIX), BF16), vm((ns, PIX), BF16),
-        vm((2, 32, 128), F32), vm((2, 32, 128), F32), vm((2, 32, 128), F32), vm((2, 32, 128), F32),
-    ]
-    for n in (nq, ns):
-        scratch += [
-            vm((C, n), F32), vm((C, n), BF16), vm((256, n), BF16), vm((256, n), BF16), vm((3, 64, n), BF16),
-            vm((64, n), BF16), vm((3, 16, n), BF16),
-        ]
+        vm((C, PIX), BF16), vm((C, PIX), BF16), vm((128, 128), BF16), vm((16, 64, 128), BF16), vm((128, 128), BF16),
+        vm((192, 128), BF16), vm((4, 160, 256), BF16), vm((192, 384), BF16), vm((nq, PIX), BF16), vm((4 * ns, PIX), BF16),
+        vm((2, 32, 128), F32), vm((2, 32, 128), F32),
+        vm((C, nq), F32), vm((C, nq), BF16), vm((256, nq), BF16), vm((256, nq), BF16), vm((3, 64, nq), BF16),
+        vm((64, nq), BF16), vm((3, 16, nq), BF16),
+        vm((128, 1024), F32), vm((128, 1024), BF16), vm((64, 1024), BF16), vm((64, 1024), BF16),
+        vm((3, 16, 1024), BF16), vm((4, 16, 256), BF16), vm((4, 16, 256), BF16),
+    ]
     scratch += [vm((128, 256), BF16), vm((16, ns), F32), vm((9, 16, HID), F32)]
     dma = pltpu.SemaphoreType.DMA
-    scratch += [dma((8,)), dma((2, 15)), dma((2, N_CHAN)), dma((8,)), dma((8,)), dma((2, 7)), dma((2, 7))]
+    scratch += [dma((8,)), dma((2, 15)), dma((2, N_CHAN)), dma((8,)), dma((8,)), dma((20,)), dma((16, 3)), dma((3,)), dma((4,))]
+    scratch += [dma((2, 8)), dma((2, 8))]
     gf, gs, gq = pl.pallas_call(
         kernel,
         out_shape=(
@@ -367,11 +468,11 @@
         ),
         name="backward",
     )(
-        features.reshape(128, 256),
-        pre_act.reshape(128, 128),
-        cotangent.reshape(128, 128),
-        w_strided.reshape(ns, C),
-        w_square.reshape(nq, C),
+        hbm(features.reshape(128, 256)),
+        hbm(pre_act.reshape(128, 128)),
+        hbm(cotangent.reshape(128, 128)),
+        hbm(w_strided.reshape(ns, C)),
+        hbm(w_square.reshape(nq, C)),
     )
     grad_features = gf.reshape(features.shape)
     strided = jnp.transpose(gs.reshape(16, 4, 4, CIN), (1, 2, 3, 0))

time: 58.1 us -> 51.7 us (0.89)
  the two profiles are of different devices: /device:TPU:32 before, /device:TPU:24 now
where the time goes in v2:
time: 51.7 us; the launch traced here: 51.6 us
  Pallas kernels  48.9 us (95%)
  local copies, waits for them, and re-layouts  2.02 us (4%)
  between operations  0.64 us (1%)
    pallas_call x1, Pallas kernels, body(): pl.pallas_call(kernel, out_shape=(jax.ShapeDtypeStruct((128, 256), BF16),...  48.9 us
    unnamed x2, local copies, waits for them, and re-layouts  1.26 us

profile of v2, /device:TPU:24, one launch (start us, length us, event | category | flops | bytes accessed | tf_op | source)
XLA Modules:
  0.0 51.6 jit_solution(2443584994140361259)
XLA Ops:
  0.6 48.9 %backward.1 = (bf16[128,256]{1,0:T(8,128)(2,1)S(1)}, f32[16,256]{1,0:T(8,128)S(1)}, f32[9,16,32]{2,1,0:T(8,128)S(1)}) custom-call(bf16[128,256]{1,0:T(8,128)(2,1)} %bitcast.17, bf16[128,128]{1,0:T(8,128)(2,1)} %bitcast.18, bf16[128,128]{1,0:T(8,128)(2,1)} %bitcast.19, bf16[256,512]{1,0:T(8,128)(2,1)} %bitcast.15, bf16[288,512]{1,0:T(8,128)(2,1)} %bitcast.14), custom_call_target="tpu_custom_call" | custom-call | tf_op jit(solution)/shard_map/backward/pallas_call | solution.py:456
  49.6 0.8 %copy.9 = f32[16,256]{0,1:T(8,128)} copy(f32[16,256]{1,0:T(8,128)S(1)} %get-tuple-element.7) | data formatting | bytes 32768 | tf_op jit(solution)/shard_map/reshape | solution.py:478
  50.3 0.6 %copy.12 = bf16[1,16,8,256]{3,2,1,0:T(8,128)(2,1)} copy(bf16[1,16,8,256]{3,2,1,0:T(8,128)(2,1)S(1)} %bitcast.13) | data formatting | bytes 131072
  51.0 0.6 %copy.13 = f32[3,3,32,16]{2,3,1,0:T(8,128)} copy(f32[3,3,32,16]{2,3,1,0:T(8,128)S(1)} %bitcast.12) | data formatting | bytes 36864

commit v3 on v2

--- a/solution.py
+++ b/solution.py
@@ -60,13 +60,12 @@
 
 def kernel(
     feat_hbm, pre_hbm, cot_hbm, ws_hbm, wq_hbm,
-    gf_hbm, gs_hbm, gq_hbm,
+    gf_v, gs_v, gq_v,
     feat_v, pre_v, cot_v, ws_v, wq_v,
     cotg, hidg, cot_t, edge, pre_t, ax, fx, a_sel, ab, fb,
     gf_send, gf_recv,
     q_own, q1, q1r, q2, q2r, q3, q3r,
     s_own, s1, s1r, s2, s2r, s3, s3r,
-    gf_v, gs_v, gq_v,
     local_sem, gat_send, gat_recv, halo_ssem, halo_rsem, edge_ssem, edge_rsem, fx_ssem, fx_rsem, rs_ssem, rs_rsem,
 ):
     r, h = lax.axis_index("row"), lax.axis_index("chan")
@@ -186,6 +185,9 @@
         send(fx.at[z, pl.ds(128, CIN)], fx.at[z, pl.ds(0, CIN)], halo_ssem.at[3], halo_rsem.at[3], down),
     ]
     gather_forward(put, take)
+    fx_rows = fx.at[z, pl.ds(CIN, 128)]
+    for k, dev in enumerate(z_peers):
+        send(fx_rows, fx_rows, fx_ssem.at[k], fx_rsem.at[z, 0], dev)
     for k in range(4):
         b = (z + k) % 4 * 4 + x
         for side in range(2):
@@ -201,11 +203,12 @@
 
     for c in halo:
         c.wait_recv()
-    fxm = fx.at[z]
-    fxm[:CIN] = masked(first, fxm[:CIN])
-    fxm[CIN + 128 :] = masked(last, fxm[CIN + 128 :])
-    for k, (p, dev) in enumerate(zip(z_ids, z_peers)):
-        send(fxm, fxm, fx_ssem.at[k], fx_rsem.at[z], dev)
+    fx[z, :CIN] = masked(first, fx[z, :CIN])
+    fx[z, CIN + 128 :] = masked(last, fx[z, CIN + 128 :])
+    for n, lo in enumerate((0, CIN + 128)):
+        rim = fx.at[z, pl.ds(lo, CIN)]
+        for k, dev in enumerate(z_peers):
+            send(rim, rim, fx_ssem.at[3 + 3 * n + k], fx_rsem.at[z, 1 + n], dev)
 
     shifts = one_hot((OW, 3 * OW), lambda i, j: (i, j % OW + j // OW - 1))
     a_sel[...] = mm(ax[...], shifts).astype(BF16)
@@ -300,7 +303,9 @@
 
         @pl.when(z != zz)
         def _():
-            copy(fx.at[zz], fx.at[zz], fx_ssem.at[0], fx_rsem.at[zz], (r, h)).wait_recv()
+            for n, (lo, size) in enumerate(((CIN, 128), (0, CIN), (CIN + 128, CIN))):
+                ref = fx.at[zz, pl.ds(lo, size)]
+                copy(ref, ref, fx_ssem.at[0], fx_rsem.at[zz, n], (r, h)).wait_recv()
 
         f_sel = mm(fx[zz], strides).astype(BF16)
         for ky in range(4):
@@ -399,14 +404,10 @@
     by_channel = one_hot((128, 128), lambda i, j: (j, (i % 8) * CIN + i // 8))
     woven = mm(phased, weave).astype(BF16)
     gf_v[...] = mm(by_channel, woven).astype(BF16)
-    out_gf = pltpu.make_async_copy(gf_v, gf_hbm, local_sem.at[5])
-    out_gf.start()
 
     gq = step_end(q_cs, q_own, q3r)
     for t in range(9):
         gq_v[t] = gq[:, t * HID : (t + 1) * HID]
-    out_gq = pltpu.make_async_copy(gq_v, gq_hbm, local_sem.at[6])
-    out_gq.start()
     last_recvs = [
         copy(s3.at[0], s3r.at[p], rs_ssem.at[1, 4], rs_rsem.at[1, 4 + p], dev) for p, dev in zip(giver_ids, givers)
     ]
@@ -420,18 +421,13 @@
     total = s3r[0].astype(F32)
     for p in range(1, 4):
         total = total + s3r[p].astype(F32)
-    gs_v[...] = total * scale
-    out_gs = pltpu.make_async_copy(gs_v, gs_hbm, local_sem.at[7])
-    out_gs.start()
+    gs_v[...] = (total * scale).T
     @pl.when(jnp.logical_not(keeps))
     def _():
         last_sends[0].wait_send()
 
     for c in sent + last_sends[1:]:
         c.wait_send()
-    out_gf.wait()
-    out_gq.wait()
-    out_gs.wait()
 
 
 def body(features, pre_act, cotangent, w_strided, w_square):
@@ -449,19 +445,18 @@
         vm((128, 1024), F32), vm((128, 1024), BF16), vm((64, 1024), BF16), vm((64, 1024), BF16),
         vm((3, 16, 1024), BF16), vm((4, 16, 256), BF16), vm((4, 16, 256), BF16),
     ]
-    scratch += [vm((128, 256), BF16), vm((16, ns), F32), vm((9, 16, HID), F32)]
     dma = pltpu.SemaphoreType.DMA
-    scratch += [dma((8,)), dma((2, 15)), dma((2, N_CHAN)), dma((8,)), dma((8,)), dma((20,)), dma((16, 3)), dma((3,)), dma((4,))]
+    scratch += [dma((8,)), dma((2, 15)), dma((2, N_CHAN)), dma((8,)), dma((8,)), dma((20,)), dma((16, 3)), dma((9,)), dma((4, 3))]
     scratch += [dma((2, 8)), dma((2, 8))]
     gf, gs, gq = pl.pallas_call(
         kernel,
         out_shape=(
             jax.ShapeDtypeStruct((128, 256), BF16),
-            jax.ShapeDtypeStruct((16, ns), F32),
+            jax.ShapeDtypeStruct((ns, 16), F32),
             jax.ShapeDtypeStruct((9, 16, HID), F32),
         ),
         in_specs=[any_spec] * 5,
-        out_specs=[any_spec] * 3,
+        out_specs=[pl.BlockSpec(memory_space=pltpu.VMEM)] * 3,
         scratch_shapes=scratch,
         compiler_params=pltpu.CompilerParams(
             collective_id=0, has_side_effects=True, vmem_limit_bytes=40 * 2**20
@@ -475,7 +470,7 @@
         hbm(w_square.reshape(nq, C)),
     )
     grad_features = gf.reshape(features.shape)
-    strided = jnp.transpose(gs.reshape(16, 4, 4, CIN), (1, 2, 3, 0))
+    strided = gs.reshape(4, 4, CIN, 16)
     square = jnp.transpose(gq.reshape(3, 3, 16, HID), (0, 1, 3, 2))
     return grad_features, strided, square
 

time: 51.7 us -> 50.3 us (0.973)
  Pallas kernels: 48.9 us -> 47.5 us
    pallas_call x1, Pallas kernels: 48.9 us -> 47.5 us  [body(): pl.pallas_call(kernel, out_shape=(jax.ShapeDtypeStruct((128, 256), BF16),...]
    reshape x1 -> x0, local copies, waits for them, and re-layouts: 0.76 us -> none  [body(): strided = jnp.transpose(gs.reshape(16, 4, 4, CIN), (1, 2, 3, 0))]
    unnamed x2 -> x3, local copies, waits for them, and re-layouts: 1.26 us -> 1.92 us
where the time goes in v3:
time: 50.3 us; the launch traced here: 50.1 us
  Pallas kernels  47.5 us (94%)
  local copies, waits for them, and re-layouts  1.92 us (4%)
  between operations  0.64 us (1%)
    pallas_call x1, Pallas kernels, body(): pl.pallas_call(kernel, out_shape=(jax.ShapeDtypeStruct((128, 256), BF16),...  47.5 us
    unnamed x3, local copies, waits for them, and re-layouts  1.92 us

profile of v3, /device:TPU:24, one launch (start us, length us, event | category | flops | bytes accessed | tf_op | source)
XLA Modules:
  0.0 50.1 jit_solution(16655380349050599138)
XLA Ops:
  0.6 47.5 %backward.1 = (bf16[128,256]{1,0:T(8,128)(2,1)S(1)}, f32[256,16]{1,0:T(8,128)S(1)}, f32[9,16,32]{2,1,0:T(8,128)S(1)}) custom-call(bf16[128,256]{1,0:T(8,128)(2,1)} %bitcast.15, bf16[128,128]{1,0:T(8,128)(2,1)} %bitcast.16, bf16[128,128]{1,0:T(8,128)(2,1)} %bitcast.17, bf16[256,512]{1,0:T(8,128)(2,1)} %bitcast.14, bf16[288,512]{1,0:T(8,128)(2,1)} %bitcast.13), custom_call_target="tpu_custom_call" | custom-call | tf_op jit(solution)/shard_map/backward/pallas_call | solution.py:451
  48.2 0.6 %copy.11 = bf16[1,16,8,256]{3,2,1,0:T(8,128)(2,1)} copy(bf16[1,16,8,256]{3,2,1,0:T(8,128)(2,1)S(1)} %bitcast.12) | data formatting | bytes 131072
  48.8 0.7 %copy.12 = f32[4,4,16,16]{3,2,1,0:T(8,128)} copy(f32[4,4,16,16]{3,2,1,0:T(8,128)S(1)} %bitcast.10) | data formatting | bytes 32768
  49.5 0.6 %copy.13 = f32[3,3,32,16]{2,3,1,0:T(8,128)} copy(f32[3,3,32,16]{2,3,1,0:T(8,128)S(1)} %bitcast.11) | data formatting | bytes 36864

commit v4 on v3

--- a/solution.py
+++ b/solution.py
@@ -142,7 +142,7 @@
             ref = block(buf, b)
             copy(ref, ref, gat_send.at[n, 0], gat_recv.at[n, b], (r, h)).wait_recv()
 
-        firsts = z_peers[1:] + x_peers + [z_peers[0]] + next_plane if n == 0 else x_peers + z_peers[1:] + [z_peers[0]] + next_plane
+        firsts = z_peers[1:] + x_peers + [z_peers[0]] + next_plane
         for dev in firsts:
             put(h, dev)
         return put, take

time: 50.3 us -> 50.4 us (level)
  no operation moved by 1% of the time
where the time goes in v4:
time: 50.4 us; the launch traced here: 50.1 us
  Pallas kernels  47.5 us (94%)
  local copies, waits for them, and re-layouts  1.92 us (4%)
  between operations  0.64 us (1%)
    pallas_call x1, Pallas kernels, body(): pl.pallas_call(kernel, out_shape=(jax.ShapeDtypeStruct((128, 256), BF16),...  47.5 us
    unnamed x3, local copies, waits for them, and re-layouts  1.92 us

profile of v4, /device:TPU:24, one launch (start us, length us, event | category | flops | bytes accessed | tf_op | source)
XLA Modules:
  0.0 50.1 jit_solution(17856206958320622562)
XLA Ops:
  0.6 47.5 %backward.1 = (bf16[128,256]{1,0:T(8,128)(2,1)S(1)}, f32[256,16]{1,0:T(8,128)S(1)}, f32[9,16,32]{2,1,0:T(8,128)S(1)}) custom-call(bf16[128,256]{1,0:T(8,128)(2,1)} %bitcast.15, bf16[128,128]{1,0:T(8,128)(2,1)} %bitcast.16, bf16[128,128]{1,0:T(8,128)(2,1)} %bitcast.17, bf16[256,512]{1,0:T(8,128)(2,1)} %bitcast.14, bf16[288,512]{1,0:T(8,128)(2,1)} %bitcast.13), custom_call_target="tpu_custom_call" | custom-call | tf_op jit(solution)/shard_map/backward/pallas_call | solution.py:451
  48.2 0.6 %copy.11 = bf16[1,16,8,256]{3,2,1,0:T(8,128)(2,1)} copy(bf16[1,16,8,256]{3,2,1,0:T(8,128)(2,1)S(1)} %bitcast.12) | data formatting | bytes 131072
  48.8 0.7 %copy.12 = f32[4,4,16,16]{3,2,1,0:T(8,128)} copy(f32[4,4,16,16]{3,2,1,0:T(8,128)S(1)} %bitcast.10) | data formatting | bytes 32768
  49.5 0.6 %copy.13 = f32[3,3,32,16]{2,3,1,0:T(8,128)} copy(f32[3,3,32,16]{2,3,1,0:T(8,128)S(1)} %bitcast.11) | data formatting | bytes 36864
